TPU v7x, 512 devices: a whole 4x4x16 slice. The times are simulated.
512 devices in a mesh: past: 8 (over y, core), second: 64 (over z, x).
Axes of the slice: x: 4, y: 4, z: 16, core: 2. Of those that a mesh axis runs over, the one named last changes fastest.
Arguments:
- green_row: float32 [1024, 64, 128], P('second'), may hold values from -4 to 4
- green_hist: float32 [32, 1024, 64, 128], P('past', 'second'), may hold values from -5.25 to 5.25, as said below
- hamiltonian: float32 [64, 128], replicated, may hold values from -0.75 to 0.75
- quad_table: float32 [8], replicated, may hold values from 0.2 to 2
- weight_index: int32 [32], P('past'), may hold values from 0 to 7
- block_start: int32 [1], replicated, may hold values from 0 to 992
Outputs:
- green_next: float32 [1024, 64, 128], P('second')
- change_norm: float32 [1], replicated
Inputs may be any that keep to these rules, and one draw needn't show every extreme that they name: `green_hist`: real numbers of order one; magnitudes differ between second times.
All inputs are finite; a program needn't handle non-finite values.
Results may differ from a plain program's by a relative error of at most 0.0003.
Values sent between devices are 32-bit elements; how exact they have to be, the bound alone decides.
A program may use at most 64 MiB of HBM per device.

v0:
```python
import math
import jax
import jax.numpy as jnp
from jax import lax
from jax.sharding import PartitionSpec as P

coupling = 0.5
step_size = 0.25


def rotate(tiles, orbits):
    return jnp.concatenate([-tiles[..., orbits:], tiles[..., :orbits]], axis=-1)


def self_energy(tiles, orbits):
    magnitude = tiles[..., :orbits] ** 2 + tiles[..., orbits:] ** 2
    return -coupling * jnp.concatenate([magnitude, magnitude], axis=-1) * tiles


def local(green_row, green_hist, hamiltonian, quad_table, weight_index, block_start):
    orbits = hamiltonian.shape[0]
    sec_rows = green_row.shape[0]
    past_rows = green_hist.shape[0]
    total_past = past_rows * lax.axis_size("past")
    window_start = block_start[0]
    offset = lax.axis_index("second") * sec_rows
    past_first = lax.axis_index("past") * past_rows
    weights = jnp.take(quad_table, weight_index, axis=0)
    norm_scale = 1.0 / math.sqrt(orbits * total_past)
    ham_real = hamiltonian[:, :orbits]
    ham_imag = hamiltonian[:, orbits:]
    herm_real = 0.5 * (ham_real + ham_real.T)
    herm_imag = 0.5 * (ham_imag - ham_imag.T)
    right_side = jnp.stack([green_hist, self_energy(green_hist, orbits)])

    def select(tiles_in, wanted):
        local_pos = wanted - offset
        inside = (local_pos >= 0) & (local_pos < sec_rows)
        picked = jnp.take(tiles_in, jnp.clip(local_pos, 0, sec_rows - 1), axis=0)
        return jnp.where(inside[:, None, None], picked, jnp.zeros_like(picked))

    def window_of(tiles_in):
        wanted = window_start + jnp.arange(total_past, dtype=jnp.int32)
        every_tile = lax.psum(select(tiles_in, wanted), "second")
        return lax.dynamic_slice_in_dim(every_tile, past_first, past_rows, 0)

    def memory(tiles_in):
        window = window_of(tiles_in)
        weight_col = weights[:, None, None]
        left_side = jnp.stack([weight_col * self_energy(window, orbits), weight_col * window])
        left_side = jnp.stack([left_side[..., :orbits], left_side[..., orbits:]])
        contracted = jnp.einsum(
            "cqpij,qpsjk->csik", left_side, right_side, precision=lax.Precision.HIGHEST
        )
        return norm_scale * (contracted[0] + rotate(contracted[1], orbits))

    def derive(tiles_in, integral):
        first = jnp.einsum("ij,sjk->sik", herm_real, tiles_in, precision=lax.Precision.HIGHEST)
        second = jnp.einsum(
            "ij,sjk->sik", herm_imag, rotate(tiles_in, orbits), precision=lax.Precision.HIGHEST
        )
        combined = first + second + integral
        return jnp.concatenate([combined[..., orbits:], -combined[..., :orbits]], axis=-1)

    def summed(tiles_in):
        return lax.psum(memory(tiles_in), "past")

    slope_one = derive(green_row, summed(green_row))
    predicted = green_row + step_size * slope_one
    slope_two = derive(predicted, summed(predicted))
    green_next = green_row + 0.5 * step_size * (slope_one + slope_two)
    square_sum = lax.psum(jnp.sum((green_next - predicted) ** 2), "second")
    entry_count = sec_rows * lax.axis_size("second") * orbits * 2 * orbits
    change = jnp.sqrt(square_sum / entry_count) / step_size
    return (green_next, change.reshape(1))


def solution(mesh):
    placed = (P("second", None, None), P("past", "second", None, None), P(), P(), P("past"), P())
    return jax.shard_map(
        local, mesh=mesh, in_specs=placed, out_specs=(P("second", None, None), P()), check_vma=False
    )
```

profile of v0, /device:TPU:8, one launch (start us, length us, event | category | flops | bytes accessed | tf_op | source)
XLA Modules:
  0.0 879.2 jit_solution(6266481443964720765)
XLA Ops:
  7.2 0.0 copy-start
  7.2 0.0 all-reduce.5.cloned.1.call-start
  7.9 1.7 gather_fusion.1
  9.6 0.0 copy-start.11
  9.6 0.0 copy-start.1
  9.6 1.2 select_select_fusion.1
  10.8 0.0 all-reduce.5.cloned.1.call-update
  10.8 0.0 all-reduce.7.cloned.1.call-start
  10.9 0.0 copy-done.11
  10.9 0.0 copy-done
  10.9 0.6 gather_fusion
  11.6 0.0 copy-done.1
  11.6 1.0 slice_negate_fusion.5
  12.5 0.0 copy-done.2
  12.5 0.6 fusion.2
  13.1 2.7 copy_bitcast_fusion
  15.8 273.4 %all-reduce.5.cloned.1.call-done = f32[32,64,128]{2,1,0:T(8,128)} async-done(((f32[32,64,128]{2,1,0:T(8,128)}), f32[32,64,128]{2,1,0:T(8,128)}) %all-reduce.5.cloned.1.call-update) | async-done | bytes 1048592 | tf_op jit(solution)/shard_map/psum | solution.py:44
  289.2 1.1 fusion.28
  290.3 1.0 fusion.31
  291.3 0.1 maximum_bitcast_fusion.10
  291.5 4.4 fusion.5
  296.0 0.0 copy-start.10
  296.0 0.0 copy-start.8
  296.0 0.2 slice_negate_fusion.4
  296.2 1.0 fusion.14
  297.2 0.0 all-reduce.7.cloned.1.call-update
  297.2 0.0 all-reduce.9.cloned.1.call-start
  297.3 0.0 copy-done.10
  297.3 0.1 fusion.61
  297.4 0.1 copy.21
  297.4 0.1 copy.40
  297.5 0.0 copy-done.8
  297.5 0.7 convolution_bitcast_fusion
  298.3 67.6 %all-reduce.7.cloned.1.call-done = f32[16,64,128]{2,1,0:T(8,128)} async-done(((f32[16,64,128]{2,1,0:T(8,128)}), f32[16,64,128]{2,1,0:T(8,128)}) %all-reduce.7.cloned.1.call-update) | async-done | bytes 524304 | tf_op jit(solution)/shard_map/psum | solution.py:66
  365.9 1.6 fusion.8
  367.6 0.2 fusion.60
  367.8 0.0 copy-start.4
  367.8 0.0 copy-start.6
  367.8 0.8 copy-done.4
  368.6 0.2 copy-done.6
  368.8 0.2 multiply_add_fusion
  369.0 0.6 gather_fusion.2
  369.6 1.2 select_select_fusion
  370.8 0.0 all-reduce.9.cloned.1.call-update
  370.8 0.0 all-reduce.11.cloned.1.call-start
  370.9 1.4 fusion.38
  372.3 273.5 %all-reduce.9.cloned.1.call-done = f32[32,64,128]{2,1,0:T(8,128)} async-done(((f32[32,64,128]{2,1,0:T(8,128)}), f32[32,64,128]{2,1,0:T(8,128)}) %all-reduce.9.cloned.1.call-update) | async-done | bytes 1048592 | tf_op jit(solution)/shard_map/psum | solution.py:44
  645.8 1.1 fusion.27
  646.8 1.0 fusion.34
  647.9 0.1 maximum_bitcast_fusion.9
  648.0 0.0 copy-done.3
  648.0 4.1 fusion.6
  652.2 0.2 slice_negate_fusion.1
  652.4 1.0 fusion.12
  653.4 0.0 all-reduce.11.cloned.1.call-update
  653.5 0.2 slice_negate_fusion.2
  653.7 68.5 %all-reduce.11.cloned.1.call-done = f32[16,64,128]{2,1,0:T(8,128)} async-done(((f32[16,64,128]{2,1,0:T(8,128)}), f32[16,64,128]{2,1,0:T(8,128)}) %all-reduce.11.cloned.1.call-update) | async-done | bytes 524304 | tf_op jit(solution)/shard_map/psum | solution.py:66
  722.2 0.0 copy-done.9
  722.2 1.9 fusion.10
  724.1 0.2 fusion.59
  724.3 0.0 copy-done.5
  724.3 0.0 copy-done.7
  724.3 1.8 multiply_reduce_fusion
  726.1 144.7 %psum.39 = f32[]{:T(128)} all-reduce(f32[]{:T(128)} %get-tuple-element.3), channel_id=1, replica_groups=mesh['past'=8,'second'=64] {'second'}, use_global_device_ids=true, to_apply=%region_5.7 | all-reduce | flops 1 | bytes 8 | tf_op jit(solution)/shard_map/psum | solution.py:72
  (12 shorter events, 0.1 us)
Async XLA Ops:
  7.2 3.7 copy-start
  7.2 282.0 %all-reduce.5.cloned.1.call-start = ((), (), s32[]{:S(2)}) async-start(), calls=%async_computation | async-start | bytes 2097152 | tf_op jit(solution)/shard_map/psum | solution.py:44
  9.6 1.3 copy-start.11
  9.6 2.0 copy-start.1
  10.8 1.7 copy-start.2
  10.8 355.1 %all-reduce.7.cloned.1.call-start = ((), (), s32[]{:S(2)}) async-start(), calls=%async_computation.1 | async-start | bytes 1048576 | tf_op jit(solution)/shard_map/psum | solution.py:66
  296.0 1.3 copy-start.10
  296.0 1.6 copy-start.8
  297.2 348.5 %all-reduce.9.cloned.1.call-start = ((), (), s32[]{:S(2)}) async-start(), calls=%async_computation.2 | async-start | bytes 2097152 | tf_op jit(solution)/shard_map/psum | solution.py:44
  367.8 0.8 copy-start.4
  367.8 1.0 copy-start.6
  370.8 277.2 %copy-start.3 = (f32[1,4,16,64,128]{4,3,0,1,2:T(8,128)S(1)}, f32[1,4,16,64,128]{4,3,0,1,2:T(8,128)}, u32[]{:S(2)}) copy-start(f32[1,4,16,64,128]{4,3,0,1,2:T(8,128)} %get-tuple-element.7) | copy-start | bytes 6291460
  370.8 351.4 %all-reduce.11.cloned.1.call-start = ((), (), s32[]{:S(2)}) async-start(), calls=%async_computation.3 | async-start | bytes 1048576 | tf_op jit(solution)/shard_map/psum | solution.py:66
  652.4 69.8 %copy-start.9 = (f32[16,128,64]{1,2,0:T(8,128)S(1)}, f32[16,128,64]{1,2,0:T(8,128)}, u32[]{:S(2)}) copy-start(f32[16,128,64]{1,2,0:T(8,128)} %fusion.38) | copy-start | bytes 1572868
  722.2 2.1 copy-start.5
  722.2 2.1 copy-start.7
Sparse Core Ops, SparseCore 0:
  11.4 277.7 all-reduce.4
  297.4 68.5 all-reduce.6
  370.9 274.7 all-reduce.8
  653.6 68.5 all-reduce.10
where the time goes:
time: 880 us; the launch traced here: 879 us
  waiting for transfers between devices  683 us (78%)
  blocking collectives  145 us (16%)
  between operations  16.5 us (2%)
  other arithmetic  16.1 us (2%)
  matrix products  14.3 us (2%)
    psum x2, waiting for transfers between devices, window_of(): every_tile = lax.psum(select(tiles_in, wanted), 'second')  547 us
    psum x1, blocking collectives, local(): square_sum = lax.psum(jnp.sum((green_next - predicted) ** 2), 'second')  145 us
    psum x2, waiting for transfers between devices, summed(): return lax.psum(memory(tiles_in), 'past')  136 us
  transfers between devices with their start and end apart: 4, of which 4 were waited for; matrix products, arithmetic and copies ran while one was open for 1% of the time, Pallas kernels for 0%

commit v1 on v0

--- a/solution.py
+++ b/solution.py
@@ -63,7 +63,7 @@
         return jnp.concatenate([combined[..., orbits:], -combined[..., :orbits]], axis=-1)
 
     def summed(tiles_in):
-        return lax.psum(memory(tiles_in), "past")
+        return jnp.sum(lax.all_gather(memory(tiles_in), "past"), axis=0)
 
     slope_one = derive(green_row, summed(green_row))
     predicted = green_row + step_size * slope_one

time: 880 us -> 816 us (0.927)
  waiting for transfers between devices: 683 us -> 613 us
    psum x2 -> x0, waiting for transfers between devices: 136 us -> none  [summed(): return lax.psum(memory(tiles_in), 'past')]
    all_gather x0 -> x2, waiting for transfers between devices: none -> 64.8 us  [summed(): return jnp.sum(lax.all_gather(memory(tiles_in), 'past'), axis=0)]
where the time goes in v1:
time: 816 us
  waiting for transfers between devices  613 us (75%)
  blocking collectives  145 us (18%)
  other arithmetic  23.4 us (3%)
  between operations  16.5 us (2%)
  matrix products  11.2 us (1%)
    psum x2, waiting for transfers between devices, window_of(): every_tile = lax.psum(select(tiles_in, wanted), 'second')  548 us
    psum x1, blocking collectives, local(): square_sum = lax.psum(jnp.sum((green_next - predicted) ** 2), 'second')  145 us
    all_gather x2, waiting for transfers between devices, summed(): return jnp.sum(lax.all_gather(memory(tiles_in), 'past'), axis=0)  64.8 us
  transfers between devices with their start and end apart: 4, of which 4 were waited for; matrix products, arithmetic and copies ran while one was open for 1% of the time, Pallas kernels for 0%

profile of v1, /device:TPU:8, one launch (start us, length us, event | category | flops | bytes accessed | tf_op | source)
XLA Modules:
  0.0 815.7 jit_solution(17675886641032141502)
XLA Ops:
  7.2 0.0 copy-start
  7.2 0.0 all-reduce.3.cloned.1.call-start
  7.9 2.6 gather_fusion.1
  10.5 2.5 select_select_fusion.1
  13.1 0.0 all-reduce.3.cloned.1.call-update
  13.1 0.0 all-gather.3.cloned.1.call-start
  13.2 0.0 copy-done.9
  13.2 0.0 copy-done
  13.2 0.6 gather_fusion
  13.8 0.0 copy-done.2
  13.8 0.6 fusion.4
  14.5 2.7 copy_bitcast_fusion
  17.1 273.9 %all-reduce.3.cloned.1.call-done = f32[32,64,128]{2,1,0:T(8,128)} async-done(((f32[32,64,128]{2,1,0:T(8,128)}), f32[32,64,128]{2,1,0:T(8,128)}) %all-reduce.3.cloned.1.call-update) | async-done | bytes 1048592 | tf_op jit(solution)/shard_map/psum | solution.py:44
  291.0 1.1 fusion.36
  292.1 1.0 fusion.39
  293.1 0.1 maximum_bitcast_fusion.2
  293.2 4.4 fusion.10
  297.7 0.0 copy-start.8
  297.7 0.0 copy-start.1
  297.8 0.2 fusion.19
  298.0 1.0 fusion.21
  299.0 0.0 all-gather.3.cloned.1.call-update
  299.0 0.0 all-reduce.5.cloned.1.call-start
  299.1 0.0 copy-done.8
  299.1 0.1 fusion.69
  299.1 0.1 copy.32
  299.2 0.1 copy.48
  299.3 0.0 copy-done.1
  299.3 0.2 slice_negate_fusion.5
  299.5 0.7 convolution_bitcast_fusion
  300.3 32.2 %all-gather.3.cloned.1.call-done = f32[8,16,64,128]{3,2,1,0:T(8,128)} async-done(((f32[1,16,64,128]{3,2,1,0:T(8,128)}), f32[8,16,64,128]{3,2,1,0:T(8,128)}) %all-gather.3.cloned.1.call-update) | async-done | bytes 4194320 | tf_op jit(solution)/shard_map/all_gather | solution.py:66
  332.5 2.6 reduce_sum.27
  335.1 0.6 fusion.14
  335.7 0.2 fusion.68
  335.9 0.0 copy-start.4
  335.9 0.0 copy-start.6
  335.9 0.8 copy-done.4
  336.7 0.2 copy-done.6
  336.9 0.2 multiply_add_fusion
  337.1 1.6 gather_fusion.2
  338.7 2.6 select_select_fusion
  341.3 0.0 all-reduce.5.cloned.1.call-update
  341.3 0.2 all-gather.5.cloned.1.call-start
  341.5 274.3 %all-reduce.5.cloned.1.call-done = f32[32,64,128]{2,1,0:T(8,128)} async-done(((f32[32,64,128]{2,1,0:T(8,128)}), f32[32,64,128]{2,1,0:T(8,128)}) %all-reduce.5.cloned.1.call-update) | async-done | bytes 1048592 | tf_op jit(solution)/shard_map/psum | solution.py:44
  615.8 1.1 fusion.35
  616.9 1.0 fusion.42
  617.9 0.1 maximum_bitcast_fusion.1
  618.1 0.0 copy-done.3
  618.1 4.1 fusion.7
  622.3 0.2 fusion.17
  622.5 1.0 fusion.18
  623.5 0.0 all-gather.5.cloned.1.call-update
  623.5 0.6 fusion.46
  624.1 0.2 slice_negate_fusion.2
  624.4 32.6 %all-gather.5.cloned.1.call-done = f32[8,16,64,128]{3,2,1,0:T(8,128)} async-done(((f32[1,16,64,128]{3,2,1,0:T(8,128)}), f32[8,16,64,128]{3,2,1,0:T(8,128)}) %all-gather.5.cloned.1.call-update) | async-done | bytes 4194320 | tf_op jit(solution)/shard_map/all_gather | solution.py:66
  657.0 2.6 reduce_sum.28
  659.6 0.0 copy-start.5
  659.6 0.0 copy-start.7
  659.6 0.8 fusion.16
  660.4 0.2 fusion.67
  660.6 0.1 copy-done.5
  660.7 0.2 copy-done.7
  660.8 1.8 multiply_reduce_fusion
  662.6 144.7 %psum.23 = f32[]{:T(128)} all-reduce(f32[]{:T(128)} %get-tuple-element.3), channel_id=1, replica_groups=mesh['past'=8,'second'=64] {'second'}, use_global_device_ids=true, to_apply=%region_5.7 | all-reduce | flops 1 | bytes 8 | tf_op jit(solution)/shard_map/psum | solution.py:72
  (10 shorter events, 0.1 us)
Async XLA Ops:
  7.2 6.0 copy-start
  7.2 283.8 %all-reduce.3.cloned.1.call-start = ((), (), s32[]{:S(2)}) async-start(), calls=%async_computation | async-start | bytes 2097152 | tf_op jit(solution)/shard_map/psum | solution.py:44
  10.5 2.6 copy-start.9
  10.5 3.3 copy-start.2
  13.1 319.4 %all-gather.3.cloned.1.call-start = ((), (), s32[]{:S(2)}) async-start(), calls=%async_computation.1 | async-start | bytes 4718592 | tf_op jit(solution)/shard_map/all_gather | solution.py:66
  297.7 1.3 copy-start.8
  297.7 1.6 copy-start.1
  299.0 316.8 %all-reduce.5.cloned.1.call-start = ((), (), s32[]{:S(2)}) async-start(), calls=%async_computation.2 | async-start | bytes 2097152 | tf_op jit(solution)/shard_map/psum | solution.py:44
  335.9 0.8 copy-start.4
  335.9 1.0 copy-start.6
  338.7 279.4 %copy-start.3 = (f32[1,4,16,64,128]{4,3,0,1,2:T(8,128)S(1)}, f32[1,4,16,64,128]{4,3,0,1,2:T(8,128)}, u32[]{:S(2)}) copy-start(f32[1,4,16,64,128]{4,3,0,1,2:T(8,128)} %get-tuple-element.7) | copy-start | bytes 6291460
  341.3 315.7 %all-gather.5.cloned.1.call-start = ((), (), s32[]{:S(2)}) async-start(), calls=%async_computation.3 | async-start | bytes 4718592 | tf_op jit(solution)/shard_map/all_gather | solution.py:66
  659.6 1.0 copy-start.5
  659.6 1.2 copy-start.7
Sparse Core Ops, SparseCore 0:
  13.2 277.7 all-reduce.2
  299.1 33.3 all-gather.2
  341.4 274.3 all-reduce.4
  623.6 33.3 all-gather.4
